TPU v7x, 512 devices: a whole 4x8x8 slice. The times are simulated.
512 devices in a mesh: space: 128 (over z, y, core), rhs: 4 (over x).
Axes of the slice: x: 4, y: 8, z: 8, core: 2. Of those that a mesh axis runs over, the one named last changes fastest.
Arguments:
- right_sides: bfloat16 [4096, 128, 128], P('space', 'rhs'), may hold values from -6 to 6
- off_blocks: bfloat16 [4096, 5, 128, 128], P('space'), may hold values from -0.1875 to 0.1875
- diag_inv: bfloat16 [4096, 128, 128], P('space')
- neighbors: int32 [4096, 5], P('space'), may hold values from 0 to 4095, as said below
- level_of: int32 [4096], replicated, may hold values from 0 to 3, as said below
Outputs:
- solution: bfloat16 [4096, 128, 128], P('space', 'rhs')
Inputs may be any that keep to these rules, and one draw needn't show every extreme that they name: `level_of`: in each device's 32 block rows no level holds more than 16 rows, and some level holds exactly 16. `neighbors`: each block column lies among the rows of the devices at most 2 indices away along space from the row's own device, and that distance 2 is reached.
All inputs are finite; a program needn't handle non-finite values.
Results may differ from a plain program's by a relative error of at most 0.0058.
Values may be sent and summed in bfloat16 or wider, within the bound.
A program may use at most 64 MiB of HBM per device.

v0:
```python
import jax
import jax.numpy as jnp
from jax import lax
from jax.sharding import PartitionSpec as P

LEVELS = 4
REACH = 2


def passed_along(block, axis, distance):
    devices = range(lax.axis_size(axis))
    route = [(i - distance, i) for i in devices if i - distance in devices]
    return lax.ppermute(block, axis, route)


def level_terms(values, off_blocks, where_from, active, running_sum):
    pieces = []
    for distance in range(REACH, -REACH - 1, -1):
        if distance == 0:
            pieces.append(values)
        else:
            pieces.append(passed_along(values, "space", distance))
    window = jnp.concatenate(pieces, axis=0)
    picked = jnp.take(window, where_from, axis=0)
    picked = picked * active[:, :, None, None].astype(jnp.bfloat16)
    return running_sum + jnp.einsum(
        "rkab,rkjb->rja", off_blocks, picked, preferred_element_type=jnp.float32
    )


def local(right_sides, off_blocks, diag_inv, neighbors, level_of):
    row_count = right_sides.shape[0]
    my_index = lax.axis_index("space")
    my_levels = lax.dynamic_slice_in_dim(level_of, my_index * row_count, row_count)
    window_index = neighbors // row_count - my_index + REACH
    where_from = window_index * row_count + neighbors % row_count
    their_level = level_of[neighbors]
    running_sum = jnp.zeros(right_sides.shape, jnp.float32)
    forward = jnp.zeros(right_sides.shape, jnp.bfloat16)
    for level_now in range(LEVELS):
        new_rows = (right_sides.astype(jnp.float32) - running_sum).astype(jnp.bfloat16)
        forward = jnp.where((my_levels == level_now)[:, None, None], new_rows, forward)
        if level_now < LEVELS - 1:
            active = (their_level == level_now) & (my_levels[:, None] > level_now)
            running_sum = level_terms(forward, off_blocks, where_from, active, running_sum)
    running_sum = jnp.zeros(right_sides.shape, jnp.float32)
    solution = jnp.zeros(right_sides.shape, jnp.bfloat16)
    for level_now in reversed(range(LEVELS)):
        reduced = (forward.astype(jnp.float32) - running_sum).astype(jnp.bfloat16)
        new_rows = jnp.einsum(
            "rab,rjb->rja", diag_inv, reduced, preferred_element_type=jnp.float32
        ).astype(jnp.bfloat16)
        solution = jnp.where((my_levels == level_now)[:, None, None], new_rows, solution)
        if level_now > 0:
            active = (their_level == level_now) & (my_levels[:, None] < level_now)
            running_sum = level_terms(solution, off_blocks, where_from, active, running_sum)
    return solution


def solution(mesh):
    in_specs = (
        P("space", "rhs", None),
        P("space", None, None, None),
        P("space", None, None),
        P("space", None),
        P(),
    )
    out_specs = P("space", "rhs", None)
    return jax.shard_map(local, mesh=mesh, in_specs=in_specs, out_specs=out_specs, check_vma=False)
```

profile of v0, /device:TPU:190, one launch (start us, length us, event | category | flops | bytes accessed | tf_op | source)
XLA Modules:
  0.0 180.7 jit_solution(10559130811768726462)
XLA Ops:
  1.9 3.5 %collective-permute-start = (bf16[32,32,128]{2,1,0:T(8,128)(2,1)S(1)}, bf16[32,32,128]{2,1,0:T(8,128)(2,1)}, u32[]{:S(2)}, u32[]{:S(2)}) collective-permute-start(bf16[32,32,128]{2,1,0:T(8,128)(2,1)S(1)} %broadcast_select_fusion), channel_id=1, source_target_pairs={{0,8},{4,12},{8,16},{12,20},{16,24},{20,28},{24,32},{28,36},{32,40... | collective-permute-start | bytes 786440 | tf_op jit(solution)/shard_map/ppermute | solution.py:13
  7.4 3.6 %collective-permute-start.2 = (bf16[32,32,128]{2,1,0:T(8,128)(2,1)S(1)}, bf16[32,32,128]{2,1,0:T(8,128)(2,1)}, u32[]{:S(2)}, u32[]{:S(2)}) collective-permute-start(bf16[32,32,128]{2,1,0:T(8,128)(2,1)S(1)} %broadcast_select_fusion), channel_id=1, source_target_pairs={{4,0},{8,4},{12,8},{16,12},{20,16},{24,20},{28,24},{32,28},{36,32}... | collective-permute-start | bytes 786440 | tf_op jit(solution)/shard_map/ppermute | solution.py:13
  11.0 2.4 %collective-permute-start.3 = (bf16[32,32,128]{2,1,0:T(8,128)(2,1)S(1)}, bf16[32,32,128]{2,1,0:T(8,128)(2,1)S(1)}, u32[]{:S(2)}, u32[]{:S(2)}) collective-permute-start(bf16[32,32,128]{2,1,0:T(8,128)(2,1)S(1)} %broadcast_select_fusion), channel_id=1, source_target_pairs={{8,0},{12,4},{16,8},{20,12},{24,16},{28,20},{32,24},{36,28},{40,32... | collective-permute-start | bytes 786440 | tf_op jit(solution)/shard_map/ppermute | solution.py:13
  19.5 5.2 %collective-permute-done.3 = bf16[32,32,128]{2,1,0:T(8,128)(2,1)S(1)} collective-permute-done((bf16[32,32,128]{2,1,0:T(8,128)(2,1)S(1)}, bf16[32,32,128]{2,1,0:T(8,128)(2,1)S(1)}, u32[]{:S(2)}, u32[]{:S(2)}) %collective-permute-start.3) | collective-permute-done | bytes 262176 | tf_op jit(solution)/shard_map/ppermute | solution.py:13
  26.6 5.6 %fusion.53 = (bf16[32,32,128]{2,1,0:T(8,128)(2,1)S(1)}, f32[32,32,128]{2,1,0:T(8,128)}) fusion(bf16[32,32,128]{2,1,0:T(8,128)(2,1)S(1)} %copy-done.3, pred[32]{0:T(512)(128)(4,1)S(1)} %get-tuple-element.23, pred[32]{0:T(512)(128)(4,1)S(1)} %get-tuple-element.26, bf16[32,5,128,128]{3,2,1,0:T(8,128)(2,1)} %param.8, bf16[32,5,32,128]{3,2,1,0:T(8,128)(2,1)} %bitcast.60, ...), kind=kOutput, calls=%fused_computation.70 | convolution fusion | flops 169738240 | bytes 7602720 | tf_op jit(solution)/shard_map/rkab,rkjb->rja/dot_general | solution.py:26
  36.3 3.6 %collective-permute-start.6 = (bf16[32,32,128]{2,1,0:T(8,128)(2,1)S(1)}, bf16[32,32,128]{2,1,0:T(8,128)(2,1)S(1)}, u32[]{:S(2)}, u32[]{:S(2)}) collective-permute-start(bf16[32,32,128]{2,1,0:T(8,128)(2,1)S(1)} %get-tuple-element.27), channel_id=1, source_target_pairs={{4,0},{8,4},{12,8},{16,12},{20,16},{24,20},{28,24},{32,28},{36,32}... | collective-permute-start | bytes 786440 | tf_op jit(solution)/shard_map/ppermute | solution.py:13
  39.9 3.9 %collective-permute-start.7 = (bf16[32,32,128]{2,1,0:T(8,128)(2,1)S(1)}, bf16[32,32,128]{2,1,0:T(8,128)(2,1)S(1)}, u32[]{:S(2)}, u32[]{:S(2)}) collective-permute-start(bf16[32,32,128]{2,1,0:T(8,128)(2,1)S(1)} %get-tuple-element.27), channel_id=1, source_target_pairs={{8,0},{12,4},{16,8},{20,12},{24,16},{28,20},{32,24},{36,28},{40,32... | collective-permute-start | bytes 786440 | tf_op jit(solution)/shard_map/ppermute | solution.py:13
  46.7 6.3 %collective-permute-done.7 = bf16[32,32,128]{2,1,0:T(8,128)(2,1)S(1)} collective-permute-done((bf16[32,32,128]{2,1,0:T(8,128)(2,1)S(1)}, bf16[32,32,128]{2,1,0:T(8,128)(2,1)S(1)}, u32[]{:S(2)}, u32[]{:S(2)}) %collective-permute-start.7) | collective-permute-done | bytes 262176 | tf_op jit(solution)/shard_map/ppermute | solution.py:13
  53.7 2.2 %gather_fusion.2 = bf16[160,32,128]{2,1,0:T(8,128)(2,1)S(1)} fusion(bf16[160,32,128]{2,1,0:T(8,128)(2,1)} %constant_dynamic-update-slice_fusion.5, s32[1024]{0:T(1024)S(1)} %pad_clamp_fusion.1), kind=kCustom, calls=%fused_computation.1.clone | custom fusion | bytes 2622080 | tf_op jit(solution)/shard_map/jit(_take)/gather | solution.py:24
  55.9 5.4 %fusion.52 = (bf16[32,32,128]{2,1,0:T(8,128)(2,1)S(1)}, f32[32,32,128]{2,1,0:T(8,128)}) fusion(bf16[32,32,128]{2,1,0:T(8,128)(2,1)S(1)} %get-tuple-element.27, bf16[32,32,128]{2,1,0:T(8,128)(2,1)S(1)} %copy-done.3, pred[32]{0:T(512)(128)(4,1)S(1)} %get-tuple-element.21, f32[32,32,128]{2,1,0:T(8,128)} %get-tuple-element.28, ...), kind=kOutput, calls=%fused_computation.69 | convolution fusion | flops 169738240 | bytes 8389120 | tf_op jit(solution)/shard_map/rkab,rkjb->rja/dot_general | solution.py:26
  61.2 2.6 %collective-permute-start.8 = (bf16[32,32,128]{2,1,0:T(8,128)(2,1)S(1)}, bf16[32,32,128]{2,1,0:T(8,128)(2,1)S(1)}, u32[]{:S(2)}, u32[]{:S(2)}) collective-permute-start(bf16[32,32,128]{2,1,0:T(8,128)(2,1)S(1)} %get-tuple-element.29), channel_id=1, source_target_pairs={{0,8},{4,12},{8,16},{12,20},{16,24},{20,28},{24,32},{28,36},{32,40... | collective-permute-start | bytes 786440 | tf_op jit(solution)/shard_map/ppermute | solution.py:13
  65.9 3.6 %collective-permute-start.10 = (bf16[32,32,128]{2,1,0:T(8,128)(2,1)S(1)}, bf16[32,32,128]{2,1,0:T(8,128)(2,1)S(1)}, u32[]{:S(2)}, u32[]{:S(2)}) collective-permute-start(bf16[32,32,128]{2,1,0:T(8,128)(2,1)S(1)} %get-tuple-element.29), channel_id=1, source_target_pairs={{4,0},{8,4},{12,8},{16,12},{20,16},{24,20},{28,24},{32,28},{36,32}... | collective-permute-start | bytes 786440 | tf_op jit(solution)/shard_map/ppermute | solution.py:13
  69.6 3.3 %collective-permute-start.11 = (bf16[32,32,128]{2,1,0:T(8,128)(2,1)S(1)}, bf16[32,32,128]{2,1,0:T(8,128)(2,1)S(1)}, u32[]{:S(2)}, u32[]{:S(2)}) collective-permute-start(bf16[32,32,128]{2,1,0:T(8,128)(2,1)S(1)} %get-tuple-element.29), channel_id=1, source_target_pairs={{8,0},{12,4},{16,8},{20,12},{24,16},{28,20},{32,24},{36,28},{40,32... | collective-permute-start | bytes 786440 | tf_op jit(solution)/shard_map/ppermute | solution.py:13
  75.7 7.8 %collective-permute-done.11 = bf16[32,32,128]{2,1,0:T(8,128)(2,1)S(1)} collective-permute-done((bf16[32,32,128]{2,1,0:T(8,128)(2,1)S(1)}, bf16[32,32,128]{2,1,0:T(8,128)(2,1)S(1)}, u32[]{:S(2)}, u32[]{:S(2)}) %collective-permute-start.11) | collective-permute-done | bytes 262176 | tf_op jit(solution)/shard_map/ppermute | solution.py:13
  84.2 2.2 %gather_fusion.3 = bf16[160,32,128]{2,1,0:T(8,128)(2,1)S(1)} fusion(bf16[160,32,128]{2,1,0:T(8,128)(2,1)} %constant_dynamic-update-slice_fusion.10, s32[1024]{0:T(1024)S(1)} %pad_clamp_fusion.1), kind=kCustom, calls=%fused_computation.2.clone | custom fusion | bytes 2622080 | tf_op jit(solution)/shard_map/jit(_take)/gather | solution.py:24
  86.4 4.6 %fusion.30 = bf16[32,32,128]{2,1,0:T(8,128)(2,1)S(1)} fusion(bf16[32,32,128]{2,1,0:T(8,128)(2,1)S(1)} %get-tuple-element.29, f32[32,32,128]{2,1,0:T(8,128)} %get-tuple-element.30, bf16[32,5,128,128]{3,2,1,0:T(8,128)(2,1)} %param.8, bf16[32,5,32,128]{3,2,1,0:T(8,128)(2,1)S(1)} %bitcast.57, pred[32,5]{1,0:T(8,128)(4,1)S(1)} %copy.12, ...), kind=kOutput, calls=%fused_computation.47 | convolution fusion | flops 169738240 | bytes 7864832 | tf_op jit(solution)/shard_map/rkab,rkjb->rja/dot_general | solution.py:26
  95.7 3.6 %collective-permute-start.14 = (bf16[32,32,128]{2,1,0:T(8,128)(2,1)S(1)}, bf16[32,32,128]{2,1,0:T(8,128)(2,1)S(1)}, u32[]{:S(2)}, u32[]{:S(2)}) collective-permute-start(bf16[32,32,128]{2,1,0:T(8,128)(2,1)S(1)} %fusion.26), channel_id=1, source_target_pairs={{4,0},{8,4},{12,8},{16,12},{20,16},{24,20},{28,24},{32,28},{36,32}... | collective-permute-start | bytes 786440 | tf_op jit(solution)/shard_map/ppermute | solution.py:13
  99.4 3.9 %collective-permute-start.15 = (bf16[32,32,128]{2,1,0:T(8,128)(2,1)S(1)}, bf16[32,32,128]{2,1,0:T(8,128)(2,1)S(1)}, u32[]{:S(2)}, u32[]{:S(2)}) collective-permute-start(bf16[32,32,128]{2,1,0:T(8,128)(2,1)S(1)} %fusion.26), channel_id=1, source_target_pairs={{8,0},{12,4},{16,8},{20,12},{24,16},{28,20},{32,24},{36,28},{40,32... | collective-permute-start | bytes 786440 | tf_op jit(solution)/shard_map/ppermute | solution.py:13
  106.2 4.8 %collective-permute-done.15 = bf16[32,32,128]{2,1,0:T(8,128)(2,1)S(1)} collective-permute-done((bf16[32,32,128]{2,1,0:T(8,128)(2,1)S(1)}, bf16[32,32,128]{2,1,0:T(8,128)(2,1)S(1)}, u32[]{:S(2)}, u32[]{:S(2)}) %collective-permute-start.15) | collective-permute-done | bytes 262176 | tf_op jit(solution)/shard_map/ppermute | solution.py:13
  111.7 2.2 %gather_fusion.4 = bf16[160,32,128]{2,1,0:T(8,128)(2,1)S(1)} fusion(bf16[160,32,128]{2,1,0:T(8,128)(2,1)} %constant_dynamic-update-slice_fusion.15, s32[1024]{0:T(1024)S(1)} %pad_clamp_fusion.1), kind=kCustom, calls=%fused_computation.3.clone | custom fusion | bytes 2622080 | tf_op jit(solution)/shard_map/jit(_take)/gather | solution.py:24
  113.8 3.9 %fusion.15 = f32[32,32,128]{2,1,0:T(8,128)S(1)} fusion(bf16[32,5,128,128]{3,2,1,0:T(8,128)(2,1)} %param.8, bf16[32,5,32,128]{3,2,1,0:T(8,128)(2,1)S(1)} %bitcast.59, pred[32,5]{1,0:T(8,128)(4,1)S(1)} %copy.12, bf16[32,5]{1,0:T(8,128)(2,1)S(1)} %and_convert_fusion.2), kind=kOutput, calls=%fused_computation.28 | convolution fusion | flops 169082880 | bytes 7078368 | tf_op jit(solution)/shard_map/rkab,rkjb->rja/dot_general | solution.py:26
  120.5 2.4 %collective-permute-start.17 = (bf16[32,32,128]{2,1,0:T(8,128)(2,1)S(1)}, bf16[32,32,128]{2,1,0:T(8,128)(2,1)S(1)}, u32[]{:S(2)}, u32[]{:S(2)}) collective-permute-start(bf16[32,32,128]{2,1,0:T(8,128)(2,1)S(1)} %fusion.27), channel_id=1, source_target_pairs={{0,4},{4,8},{8,12},{12,16},{16,20},{20,24},{24,28},{28,32},{32,36}... | collective-permute-start | bytes 786440 | tf_op jit(solution)/shard_map/ppermute | solution.py:13
  122.9 3.2 %collective-permute-start.18 = (bf16[32,32,128]{2,1,0:T(8,128)(2,1)S(1)}, bf16[32,32,128]{2,1,0:T(8,128)(2,1)S(1)}, u32[]{:S(2)}, u32[]{:S(2)}) collective-permute-start(bf16[32,32,128]{2,1,0:T(8,128)(2,1)S(1)} %fusion.27), channel_id=1, source_target_pairs={{4,0},{8,4},{12,8},{16,12},{20,16},{24,20},{28,24},{32,28},{36,32}... | collective-permute-start | bytes 786440 | tf_op jit(solution)/shard_map/ppermute | solution.py:13
  126.0 3.9 %collective-permute-start.19 = (bf16[32,32,128]{2,1,0:T(8,128)(2,1)S(1)}, bf16[32,32,128]{2,1,0:T(8,128)(2,1)S(1)}, u32[]{:S(2)}, u32[]{:S(2)}) collective-permute-start(bf16[32,32,128]{2,1,0:T(8,128)(2,1)S(1)} %fusion.27), channel_id=1, source_target_pairs={{8,0},{12,4},{16,8},{20,12},{24,16},{28,20},{32,24},{36,28},{40,32... | collective-permute-start | bytes 786440 | tf_op jit(solution)/shard_map/ppermute | solution.py:13
  132.9 10.3 %collective-permute-done.19 = bf16[32,32,128]{2,1,0:T(8,128)(2,1)S(1)} collective-permute-done((bf16[32,32,128]{2,1,0:T(8,128)(2,1)S(1)}, bf16[32,32,128]{2,1,0:T(8,128)(2,1)S(1)}, u32[]{:S(2)}, u32[]{:S(2)}) %collective-permute-start.19) | collective-permute-done | bytes 262176 | tf_op jit(solution)/shard_map/ppermute | solution.py:13
  143.9 2.2 %gather_fusion.5 = bf16[160,32,128]{2,1,0:T(8,128)(2,1)S(1)} fusion(bf16[160,32,128]{2,1,0:T(8,128)(2,1)} %constant_dynamic-update-slice_fusion.20, s32[1024]{0:T(1024)S(1)} %pad_clamp_fusion.1), kind=kCustom, calls=%fused_computation.4.clone | custom fusion | bytes 2622080 | tf_op jit(solution)/shard_map/jit(_take)/gather | solution.py:24
  146.0 4.6 %fusion.20 = f32[32,32,128]{2,1,0:T(8,128)S(1)} fusion(f32[32,32,128]{2,1,0:T(8,128)} %copy-done.2, bf16[32,5,128,128]{3,2,1,0:T(8,128)(2,1)} %param.8, bf16[32,5,32,128]{3,2,1,0:T(8,128)(2,1)S(1)} %bitcast.58, pred[32,5]{1,0:T(8,128)(4,1)S(1)} %copy.12, bf16[32,5]{1,0:T(8,128)(2,1)S(1)} %get-tuple-element.12), kind=kOutput, calls=%fused_computation.33 | convolution fusion | flops 169213952 | bytes 7602656 | tf_op jit(solution)/shard_map/rkab,rkjb->rja/dot_general | solution.py:26
  155.2 3.6 %collective-permute-start.22 = (bf16[32,32,128]{2,1,0:T(8,128)(2,1)S(1)}, bf16[32,32,128]{2,1,0:T(8,128)(2,1)S(1)}, u32[]{:S(2)}, u32[]{:S(2)}) collective-permute-start(bf16[32,32,128]{2,1,0:T(8,128)(2,1)S(1)} %fusion.28), channel_id=1, source_target_pairs={{4,0},{8,4},{12,8},{16,12},{20,16},{24,20},{28,24},{32,28},{36,32}... | collective-permute-start | bytes 786440 | tf_op jit(solution)/shard_map/ppermute | solution.py:13
  158.8 3.9 %collective-permute-start.23 = (bf16[32,32,128]{2,1,0:T(8,128)(2,1)S(1)}, bf16[32,32,128]{2,1,0:T(8,128)(2,1)S(1)}, u32[]{:S(2)}, u32[]{:S(2)}) collective-permute-start(bf16[32,32,128]{2,1,0:T(8,128)(2,1)S(1)} %fusion.28), channel_id=1, source_target_pairs={{8,0},{12,4},{16,8},{20,12},{24,16},{28,20},{32,24},{36,28},{40,32... | collective-permute-start | bytes 786440 | tf_op jit(solution)/shard_map/ppermute | solution.py:13
  165.6 6.5 %collective-permute-done.23 = bf16[32,32,128]{2,1,0:T(8,128)(2,1)S(1)} collective-permute-done((bf16[32,32,128]{2,1,0:T(8,128)(2,1)S(1)}, bf16[32,32,128]{2,1,0:T(8,128)(2,1)S(1)}, u32[]{:S(2)}, u32[]{:S(2)}) %collective-permute-start.23) | collective-permute-done | bytes 262176 | tf_op jit(solution)/shard_map/ppermute | solution.py:13
  172.9 2.2 %gather_fusion.6 = bf16[160,32,128]{2,1,0:T(8,128)(2,1)S(1)} fusion(bf16[160,32,128]{2,1,0:T(8,128)(2,1)} %constant_dynamic-update-slice_fusion.25, s32[1024]{0:T(1024)S(1)} %pad_clamp_fusion.1), kind=kCustom, calls=%fused_computation.5.clone | custom fusion | bytes 2622080 | tf_op jit(solution)/shard_map/jit(_take)/gather | solution.py:24
  175.0 5.7 %fusion.29 = bf16[32,32,128]{2,1,0:T(8,128)(2,1)} fusion(bf16[32,32,128]{2,1,0:T(8,128)(2,1)S(1)} %fusion.28, bf16[32,128,128]{2,1,0:T(8,128)(2,1)S(1)} %copy-done, f32[32,32,128]{2,1,0:T(8,128)S(1)} %fusion.20, bf16[32,5,128,128]{3,2,1,0:T(8,128)(2,1)} %param.8, bf16[32,5,32,128]{3,2,1,0:T(8,128)(2,1)S(1)} %bitcast.55, pred[32,5]{1,0:T(8,128)(4,1)S(1)} %copy.12, ...), kind=kOutput, calls=%fused_computation.46 | convolution fusion | flops 203423744 | bytes 8913408 | tf_op jit(solution)/shard_map/rab,rjb->rja/dot_general | solution.py:50
  (97 shorter events, 47.8 us)
Async XLA Ops:
  0.0 91.0 %copy-start = (bf16[32,128,128]{2,1,0:T(8,128)(2,1)S(1)}, bf16[32,128,128]{2,1,0:T(8,128)(2,1)}, u32[]{:S(2)}) copy-start(bf16[32,128,128]{2,1,0:T(8,128)(2,1)} %param.9) | copy-start | bytes 3145732
  0.0 14.3 %copy-start.1 = (s32[4096]{0:T(1024)S(1)}, s32[4096]{0:T(1024)}, u32[]{:S(2)}) copy-start(s32[4096]{0:T(1024)} %param.11) | copy-start | bytes 49156
  1.9 14.4 %collective-permute-start = (bf16[32,32,128]{2,1,0:T(8,128)(2,1)S(1)}, bf16[32,32,128]{2,1,0:T(8,128)(2,1)}, u32[]{:S(2)}, u32[]{:S(2)}) collective-permute-start(bf16[32,32,128]{2,1,0:T(8,128)(2,1)S(1)} %broadcast_select_fusion), channel_id=1, source_target_pairs={{0,8},{4,12},{8,16},{12,20},{16,24},{20,28},{24,32},{28,36},{32,40... | collective-permute-start | bytes 786440 | tf_op jit(solution)/shard_map/ppermute | solution.py:13
  5.4 11.9 %collective-permute-start.1 = (bf16[32,32,128]{2,1,0:T(8,128)(2,1)S(1)}, bf16[32,32,128]{2,1,0:T(8,128)(2,1)}, u32[]{:S(2)}, u32[]{:S(2)}) collective-permute-start(bf16[32,32,128]{2,1,0:T(8,128)(2,1)S(1)} %broadcast_select_fusion), channel_id=1, source_target_pairs={{0,4},{4,8},{8,12},{12,16},{16,20},{20,24},{24,28},{28,32},{32,36}... | collective-permute-start | bytes 786440 | tf_op jit(solution)/shard_map/ppermute | solution.py:13
  7.4 11.1 %collective-permute-start.2 = (bf16[32,32,128]{2,1,0:T(8,128)(2,1)S(1)}, bf16[32,32,128]{2,1,0:T(8,128)(2,1)}, u32[]{:S(2)}, u32[]{:S(2)}) collective-permute-start(bf16[32,32,128]{2,1,0:T(8,128)(2,1)S(1)} %broadcast_select_fusion), channel_id=1, source_target_pairs={{4,0},{8,4},{12,8},{16,12},{20,16},{24,20},{28,24},{32,28},{36,32}... | collective-permute-start | bytes 786440 | tf_op jit(solution)/shard_map/ppermute | solution.py:13
  11.0 13.6 %collective-permute-start.3 = (bf16[32,32,128]{2,1,0:T(8,128)(2,1)S(1)}, bf16[32,32,128]{2,1,0:T(8,128)(2,1)S(1)}, u32[]{:S(2)}, u32[]{:S(2)}) collective-permute-start(bf16[32,32,128]{2,1,0:T(8,128)(2,1)S(1)} %broadcast_select_fusion), channel_id=1, source_target_pairs={{8,0},{12,4},{16,8},{20,12},{24,16},{28,20},{32,24},{36,28},{40,32... | collective-permute-start | bytes 786440 | tf_op jit(solution)/shard_map/ppermute | solution.py:13
  14.3 1.7 copy-start.6
  15.8 2.5 %copy-start.3 = (bf16[32,32,128]{2,1,0:T(8,128)(2,1)S(1)}, bf16[32,32,128]{2,1,0:T(8,128)(2,1)}, u32[]{:S(2)}) copy-start(bf16[32,32,128]{2,1,0:T(8,128)(2,1)} %param.7) | copy-start | bytes 786436
  32.2 11.6 %collective-permute-start.4 = (bf16[32,32,128]{2,1,0:T(8,128)(2,1)S(1)}, bf16[32,32,128]{2,1,0:T(8,128)(2,1)S(1)}, u32[]{:S(2)}, u32[]{:S(2)}) collective-permute-start(bf16[32,32,128]{2,1,0:T(8,128)(2,1)S(1)} %get-tuple-element.27), channel_id=1, source_target_pairs={{0,8},{4,12},{8,16},{12,20},{16,24},{20,28},{24,32},{28,36},{32,40... | collective-permute-start | bytes 786440 | tf_op jit(solution)/shard_map/ppermute | solution.py:13
  34.3 10.3 %collective-permute-start.5 = (bf16[32,32,128]{2,1,0:T(8,128)(2,1)S(1)}, bf16[32,32,128]{2,1,0:T(8,128)(2,1)S(1)}, u32[]{:S(2)}, u32[]{:S(2)}) collective-permute-start(bf16[32,32,128]{2,1,0:T(8,128)(2,1)S(1)} %get-tuple-element.27), channel_id=1, source_target_pairs={{0,4},{4,8},{8,12},{12,16},{16,20},{20,24},{24,28},{28,32},{32,36}... | collective-permute-start | bytes 786440 | tf_op jit(solution)/shard_map/ppermute | solution.py:13
  36.3 9.8 %collective-permute-start.6 = (bf16[32,32,128]{2,1,0:T(8,128)(2,1)S(1)}, bf16[32,32,128]{2,1,0:T(8,128)(2,1)S(1)}, u32[]{:S(2)}, u32[]{:S(2)}) collective-permute-start(bf16[32,32,128]{2,1,0:T(8,128)(2,1)S(1)} %get-tuple-element.27), channel_id=1, source_target_pairs={{4,0},{8,4},{12,8},{16,12},{20,16},{24,20},{28,24},{32,28},{36,32}... | collective-permute-start | bytes 786440 | tf_op jit(solution)/shard_map/ppermute | solution.py:13
  39.9 13.1 %collective-permute-start.7 = (bf16[32,32,128]{2,1,0:T(8,128)(2,1)S(1)}, bf16[32,32,128]{2,1,0:T(8,128)(2,1)S(1)}, u32[]{:S(2)}, u32[]{:S(2)}) collective-permute-start(bf16[32,32,128]{2,1,0:T(8,128)(2,1)S(1)} %get-tuple-element.27), channel_id=1, source_target_pairs={{8,0},{12,4},{16,8},{20,12},{24,16},{28,20},{32,24},{36,28},{40,32... | collective-permute-start | bytes 786440 | tf_op jit(solution)/shard_map/ppermute | solution.py:13
  61.2 11.6 %collective-permute-start.8 = (bf16[32,32,128]{2,1,0:T(8,128)(2,1)S(1)}, bf16[32,32,128]{2,1,0:T(8,128)(2,1)S(1)}, u32[]{:S(2)}, u32[]{:S(2)}) collective-permute-start(bf16[32,32,128]{2,1,0:T(8,128)(2,1)S(1)} %get-tuple-element.29), channel_id=1, source_target_pairs={{0,8},{4,12},{8,16},{12,20},{16,24},{20,28},{24,32},{28,36},{32,40... | collective-permute-start | bytes 786440 | tf_op jit(solution)/shard_map/ppermute | solution.py:13
  63.9 9.6 %collective-permute-start.9 = (bf16[32,32,128]{2,1,0:T(8,128)(2,1)S(1)}, bf16[32,32,128]{2,1,0:T(8,128)(2,1)S(1)}, u32[]{:S(2)}, u32[]{:S(2)}) collective-permute-start(bf16[32,32,128]{2,1,0:T(8,128)(2,1)S(1)} %get-tuple-element.29), channel_id=1, source_target_pairs={{0,4},{4,8},{8,12},{12,16},{16,20},{20,24},{24,28},{28,32},{32,36}... | collective-permute-start | bytes 786440 | tf_op jit(solution)/shard_map/ppermute | solution.py:13
  65.9 9.1 %collective-permute-start.10 = (bf16[32,32,128]{2,1,0:T(8,128)(2,1)S(1)}, bf16[32,32,128]{2,1,0:T(8,128)(2,1)S(1)}, u32[]{:S(2)}, u32[]{:S(2)}) collective-permute-start(bf16[32,32,128]{2,1,0:T(8,128)(2,1)S(1)} %get-tuple-element.29), channel_id=1, source_target_pairs={{4,0},{8,4},{12,8},{16,12},{20,16},{24,20},{28,24},{32,28},{36,32}... | collective-permute-start | bytes 786440 | tf_op jit(solution)/shard_map/ppermute | solution.py:13
  69.6 13.9 %collective-permute-start.11 = (bf16[32,32,128]{2,1,0:T(8,128)(2,1)S(1)}, bf16[32,32,128]{2,1,0:T(8,128)(2,1)S(1)}, u32[]{:S(2)}, u32[]{:S(2)}) collective-permute-start(bf16[32,32,128]{2,1,0:T(8,128)(2,1)S(1)} %get-tuple-element.29), channel_id=1, source_target_pairs={{8,0},{12,4},{16,8},{20,12},{24,16},{28,20},{32,24},{36,28},{40,32... | collective-permute-start | bytes 786440 | tf_op jit(solution)/shard_map/ppermute | solution.py:13
  91.7 11.6 %collective-permute-start.12 = (bf16[32,32,128]{2,1,0:T(8,128)(2,1)S(1)}, bf16[32,32,128]{2,1,0:T(8,128)(2,1)S(1)}, u32[]{:S(2)}, u32[]{:S(2)}) collective-permute-start(bf16[32,32,128]{2,1,0:T(8,128)(2,1)S(1)} %fusion.26), channel_id=1, source_target_pairs={{0,8},{4,12},{8,16},{12,20},{16,24},{20,28},{24,32},{28,36},{32,40... | collective-permute-start | bytes 786440 | tf_op jit(solution)/shard_map/ppermute | solution.py:13
  93.7 10.3 %collective-permute-start.13 = (bf16[32,32,128]{2,1,0:T(8,128)(2,1)S(1)}, bf16[32,32,128]{2,1,0:T(8,128)(2,1)S(1)}, u32[]{:S(2)}, u32[]{:S(2)}) collective-permute-start(bf16[32,32,128]{2,1,0:T(8,128)(2,1)S(1)} %fusion.26), channel_id=1, source_target_pairs={{0,4},{4,8},{8,12},{12,16},{16,20},{20,24},{24,28},{28,32},{32,36}... | collective-permute-start | bytes 786440 | tf_op jit(solution)/shard_map/ppermute | solution.py:13
  95.7 9.7 %collective-permute-start.14 = (bf16[32,32,128]{2,1,0:T(8,128)(2,1)S(1)}, bf16[32,32,128]{2,1,0:T(8,128)(2,1)S(1)}, u32[]{:S(2)}, u32[]{:S(2)}) collective-permute-start(bf16[32,32,128]{2,1,0:T(8,128)(2,1)S(1)} %fusion.26), channel_id=1, source_target_pairs={{4,0},{8,4},{12,8},{16,12},{20,16},{24,20},{28,24},{32,28},{36,32}... | collective-permute-start | bytes 786440 | tf_op jit(solution)/shard_map/ppermute | solution.py:13
  99.4 11.6 %collective-permute-start.15 = (bf16[32,32,128]{2,1,0:T(8,128)(2,1)S(1)}, bf16[32,32,128]{2,1,0:T(8,128)(2,1)S(1)}, u32[]{:S(2)}, u32[]{:S(2)}) collective-permute-start(bf16[32,32,128]{2,1,0:T(8,128)(2,1)S(1)} %fusion.26), channel_id=1, source_target_pairs={{8,0},{12,4},{16,8},{20,12},{24,16},{28,20},{32,24},{36,28},{40,32... | collective-permute-start | bytes 786440 | tf_op jit(solution)/shard_map/ppermute | solution.py:13
  117.7 13.0 %copy-start.2 = (f32[32,32,128]{2,1,0:T(8,128)}, f32[32,32,128]{2,1,0:T(8,128)S(1)}, u32[]{:S(2)}) copy-start(f32[32,32,128]{2,1,0:T(8,128)S(1)} %fusion.15) | copy-start | bytes 1572868
  118.3 24.8 %copy-start.4 = (bf16[32,32,128]{2,1,0:T(8,128)(2,1)}, bf16[32,32,128]{2,1,0:T(8,128)(2,1)S(1)}, u32[]{:S(2)}) copy-start(bf16[32,32,128]{2,1,0:T(8,128)(2,1)S(1)} %fusion.27) | copy-start | bytes 786436
  118.3 11.6 %collective-permute-start.16 = (bf16[32,32,128]{2,1,0:T(8,128)(2,1)S(1)}, bf16[32,32,128]{2,1,0:T(8,128)(2,1)S(1)}, u32[]{:S(2)}, u32[]{:S(2)}) collective-permute-start(bf16[32,32,128]{2,1,0:T(8,128)(2,1)S(1)} %fusion.27), channel_id=1, source_target_pairs={{0,8},{4,12},{8,16},{12,20},{16,24},{20,28},{24,32},{28,36},{32,40... | collective-permute-start | bytes 786440 | tf_op jit(solution)/shard_map/ppermute | solution.py:13
  120.5 10.2 %collective-permute-start.17 = (bf16[32,32,128]{2,1,0:T(8,128)(2,1)S(1)}, bf16[32,32,128]{2,1,0:T(8,128)(2,1)S(1)}, u32[]{:S(2)}, u32[]{:S(2)}) collective-permute-start(bf16[32,32,128]{2,1,0:T(8,128)(2,1)S(1)} %fusion.27), channel_id=1, source_target_pairs={{0,4},{4,8},{8,12},{12,16},{16,20},{20,24},{24,28},{28,32},{32,36}... | collective-permute-start | bytes 786440 | tf_op jit(solution)/shard_map/ppermute | solution.py:13
  122.9 9.3 %collective-permute-start.18 = (bf16[32,32,128]{2,1,0:T(8,128)(2,1)S(1)}, bf16[32,32,128]{2,1,0:T(8,128)(2,1)S(1)}, u32[]{:S(2)}, u32[]{:S(2)}) collective-permute-start(bf16[32,32,128]{2,1,0:T(8,128)(2,1)S(1)} %fusion.27), channel_id=1, source_target_pairs={{4,0},{8,4},{12,8},{16,12},{20,16},{24,20},{28,24},{32,28},{36,32}... | collective-permute-start | bytes 786440 | tf_op jit(solution)/shard_map/ppermute | solution.py:13
  126.0 17.1 %collective-permute-start.19 = (bf16[32,32,128]{2,1,0:T(8,128)(2,1)S(1)}, bf16[32,32,128]{2,1,0:T(8,128)(2,1)S(1)}, u32[]{:S(2)}, u32[]{:S(2)}) collective-permute-start(bf16[32,32,128]{2,1,0:T(8,128)(2,1)S(1)} %fusion.27), channel_id=1, source_target_pairs={{8,0},{12,4},{16,8},{20,12},{24,16},{28,20},{32,24},{36,28},{40,32... | collective-permute-start | bytes 786440 | tf_op jit(solution)/shard_map/ppermute | solution.py:13
  146.0 4.6 %copy-start.5 = (bf16[32,32,128]{2,1,0:T(8,128)(2,1)S(1)}, bf16[32,32,128]{2,1,0:T(8,128)(2,1)}, u32[]{:S(2)}) copy-start(bf16[32,32,128]{2,1,0:T(8,128)(2,1)} %copy-done.4) | copy-start | bytes 786436
  151.3 11.5 %collective-permute-start.20 = (bf16[32,32,128]{2,1,0:T(8,128)(2,1)S(1)}, bf16[32,32,128]{2,1,0:T(8,128)(2,1)S(1)}, u32[]{:S(2)}, u32[]{:S(2)}) collective-permute-start(bf16[32,32,128]{2,1,0:T(8,128)(2,1)S(1)} %fusion.28), channel_id=1, source_target_pairs={{0,8},{4,12},{8,16},{12,20},{16,24},{20,28},{24,32},{28,36},{32,40... | collective-permute-start | bytes 786440 | tf_op jit(solution)/shard_map/ppermute | solution.py:13
  153.2 10.2 %collective-permute-start.21 = (bf16[32,32,128]{2,1,0:T(8,128)(2,1)S(1)}, bf16[32,32,128]{2,1,0:T(8,128)(2,1)S(1)}, u32[]{:S(2)}, u32[]{:S(2)}) collective-permute-start(bf16[32,32,128]{2,1,0:T(8,128)(2,1)S(1)} %fusion.28), channel_id=1, source_target_pairs={{0,4},{4,8},{8,12},{12,16},{16,20},{20,24},{24,28},{28,32},{32,36}... | collective-permute-start | bytes 786440 | tf_op jit(solution)/shard_map/ppermute | solution.py:13
  155.2 9.8 %collective-permute-start.22 = (bf16[32,32,128]{2,1,0:T(8,128)(2,1)S(1)}, bf16[32,32,128]{2,1,0:T(8,128)(2,1)S(1)}, u32[]{:S(2)}, u32[]{:S(2)}) collective-permute-start(bf16[32,32,128]{2,1,0:T(8,128)(2,1)S(1)} %fusion.28), channel_id=1, source_target_pairs={{4,0},{8,4},{12,8},{16,12},{20,16},{24,20},{28,24},{32,28},{36,32}... | collective-permute-start | bytes 786440 | tf_op jit(solution)/shard_map/ppermute | solution.py:13
  158.8 13.3 %collective-permute-start.23 = (bf16[32,32,128]{2,1,0:T(8,128)(2,1)S(1)}, bf16[32,32,128]{2,1,0:T(8,128)(2,1)S(1)}, u32[]{:S(2)}, u32[]{:S(2)}) collective-permute-start(bf16[32,32,128]{2,1,0:T(8,128)(2,1)S(1)} %fusion.28), channel_id=1, source_target_pairs={{8,0},{12,4},{16,8},{20,12},{24,16},{28,20},{32,24},{36,28},{40,32... | collective-permute-start | bytes 786440 | tf_op jit(solution)/shard_map/ppermute | solution.py:13
where the time goes:
time: 182 us; the launch traced here: 181 us
  starting transfers between devices  68.6 us (38%)
  waiting for transfers between devices  40.8 us (22%)
  local copies, waits for them, and re-layouts  36 us (20%)
  matrix products  31.7 us (17%)
  other arithmetic  3.11 us (2%)
    ppermute x24, starting transfers between devices, passed_along(): return lax.ppermute(block, axis, route)  68.6 us
    ppermute x24, waiting for transfers between devices, passed_along(): return lax.ppermute(block, axis, route)  40.8 us
    dot_general x5, matrix products, level_terms(): jnp.einsum('rkab,rkjb->rja', off_blocks, picked, preferred_element_type=j...  24 us
    unnamed x37, local copies, waits for them, and re-layouts  17.4 us
    gather x6, local copies, waits for them, and re-layouts, level_terms(): picked = jnp.take(window, where_from, axis=0)  12.7 us
    dot_general x4, matrix products, local(): jnp.einsum('rab,rjb->rja', diag_inv, reduced, preferred_element_type=jnp....  7.64 us
  transfers between devices with their start and end apart: 24, of which 6 were waited for; matrix products, arithmetic and copies ran while one was open for 12% of the time, Pallas kernels for 0%

commit v1 on v0

v1 whole, which is shorter than its diff:
```python
import functools

import jax
import jax.numpy as jnp
from jax import lax
from jax.experimental import pallas as pl
from jax.experimental.pallas import tpu as pltpu
from jax.sharding import PartitionSpec as P

MESH = pl.DeviceIdType.MESH
LEVELS = 4
REACH = 2
NEIGH = 5
CAP = 16
STEPS = 6
CHUNK = 4
PIECES = CAP // CHUNK
SIBLING, NEAR, FAR, PASSED, OWN = range(5)
SPAN = 5 * CAP
ZERO = STEPS * SPAN
ROW, PLACE = NEIGH, NEIGH + 1


def window(me, count, level_ref, rows):
    per_line = 128 // rows
    across = lax.broadcasted_iota(jnp.int32, (rows, rows), 1)
    down = lax.broadcasted_iota(jnp.int32, (rows, rows), 0)

    def stand(row):
        return jnp.sum(jnp.where(across == down, row, 0), axis=1, keepdims=True)

    def levels(offset):
        device = jnp.clip(me + offset, 0, count - 1)
        line = level_ref[pl.ds(device // per_line, 1), :]
        part = device % per_line
        here = jnp.zeros((1, rows), jnp.int32)
        for t in range(per_line):
            here = jnp.where(part == t, line[:, t * rows : (t + 1) * rows], here)
        here = jnp.broadcast_to(here, (rows, rows))
        return here, stand(here)

    def ranks(here, column):
        earlier = jnp.where((column == here) & (down < across), 1, 0)
        return jnp.minimum(jnp.sum(earlier, axis=0, keepdims=True), CAP - 1)

    return across, down, stand, levels, ranks


def columns():
    lane = lax.broadcasted_iota(jnp.int32, (1, 128), 1)
    number = lane // CAP
    return lane, number, jnp.where(number < 3, number + 1, 5 - number)


def fill_rows(me, count, level_ref, rows, table_ref):
    across, down, _, levels, ranks = window(me, count, level_ref, rows)
    here, column = levels(0)
    earlier = jnp.where((column == here) & (across < down), 1, 0)
    slot = column * CAP + jnp.sum(earlier, axis=1, keepdims=True)
    lane, _, solves = columns()
    place = slot == jnp.broadcast_to(solves * CAP + lane % CAP, (rows, 128))
    number = lax.broadcasted_iota(jnp.int32, (rows, 128), 0)
    row_of = jnp.sum(jnp.where(place, number, 0), axis=0, keepdims=True)
    table_ref[ROW : ROW + 1, :] = jnp.clip(row_of, 0, rows - 1)
    table_ref[PLACE : PLACE + 1, 0:rows] = jnp.clip(here[0:1, :] * CAP + ranks(here, column), 0, LEVELS * CAP - 1)
    return place


def fill_terms(me, parity, count, level_ref, neighbor_ref, rows, place, table_ref):
    across, _, stand, levels, ranks = window(me, count, level_ref, rows)
    _, number, solves = columns()
    sections = {-2: FAR - parity, -1: PASSED - 3 * parity, 0: OWN, 1: 3 * parity, 2: NEAR + parity}
    codes = []
    for offset in range(-REACH, REACH + 1):
        here, column = levels(offset)
        codes.append(here * 128 + ranks(here, column) + sections[offset] * CAP)
    for k in range(NEIGH):
        row = jnp.broadcast_to(neighbor_ref[k : k + 1, :], (rows, rows))
        which = stand(row) - (me - REACH) * rows
        found = jnp.zeros((rows, rows), jnp.int32)
        for j in range(2 * REACH + 1):
            found += jnp.where(which - j * rows == across, codes[j], 0)
        code = jnp.sum(found, axis=1, keepdims=True)
        by_slot = jnp.sum(jnp.where(place, code, 0), axis=0, keepdims=True)
        spot, level = by_slot & 127, by_slot >> 7
        lower = (number < 3) & (level < solves)
        upper = (number >= 3) & (level > solves)
        index = jnp.where(lower, level * SPAN + spot, jnp.where(upper, (STEPS - level) * SPAN + spot, ZERO))
        table_ref[k : k + 1, :] = jnp.clip(index, 0, ZERO)


def kernel(count, level_ref, neighbor_ref, right_hbm, off_hbm, inverse_hbm, out_ref,
           right, off, inverse, table_v, table, value, solved, leaving, arriving,
           load_sem, send_sem, near_sem, other_sem):
    me = lax.axis_index("space")
    parity = lax.rem(me, 2)
    sibling = me + 1 - 2 * parity
    to_near, to_far = me - 2 + 4 * parity, me + 2 - 4 * parity
    has_near = (to_near >= 0) & (to_near < count)
    has_far = (to_far >= 0) & (to_far < count)

    barrier = pltpu.get_barrier_semaphore()

    def greet(*targets):
        for target in targets:
            pl.semaphore_signal(barrier, inc=1, device_id={"space": target}, device_id_type=MESH)

    greet(sibling)
    pl.when(has_near)(lambda: greet(to_near))
    pl.when(has_far)(lambda: greet(to_far))

    rows = right.shape[0]
    load_right = pltpu.make_async_copy(right_hbm, right, load_sem.at[0])
    load_right.start()
    for start in range(0, rows, 4):
        part = pl.ds(start, 4)
        pltpu.make_async_copy(off_hbm.at[part], off.at[part], load_sem.at[1]).start()
    load_off = pltpu.make_async_copy(off_hbm, off, load_sem.at[1])
    load_inverse = pltpu.make_async_copy(inverse_hbm, inverse, load_sem.at[2])
    load_inverse.start()
    load_table = pltpu.make_async_copy(table_v, table, load_sem.at[3])

    table_v[...] = jnp.zeros_like(table_v)
    place = fill_rows(me, count, level_ref, rows, table_v)
    load_table.start()
    solved[ZERO] = jnp.zeros(solved.shape[1:], solved.dtype)

    def remote(source, target, kind, step, to, sem):
        return pltpu.make_async_remote_copy(
            src_ref=source, dst_ref=target, send_sem=send_sem.at[kind, step], recv_sem=sem,
            device_id={"space": to}, device_id_type=MESH,
        )

    def section(step, which, start=0, size=CAP):
        return arriving.at[step, pl.ds(which * CAP + start, size)]

    def own(step, start=0, size=CAP):
        return leaving.at[step, pl.ds(start, size)]

    def send_near(step, piece):
        at = piece * CHUNK

        @pl.when(has_near)
        def _():
            remote(own(step, at, CHUNK), section(step, NEAR, at, CHUNK), 1, step, to_near,
                   near_sem.at[step, piece]).start()

    def send_far(step, start, size):
        @pl.when(has_far)
        def _():
            remote(own(step, start, size), section(step, FAR, start, size), 2, step, to_far,
                   other_sem.at[step, 1]).start()

    def send_sibling(step):
        remote(own(step), section(step, SIBLING), 0, step, sibling, other_sem.at[step, 0]).start()

    def arrived(step, which, start, size, sem):
        there = section(step, which, start, size)
        remote(there, there, 0, step, sibling, sem).wait_recv()

    def keep(step, which):
        solved[pl.ds(step * SPAN + which * CAP, CAP)] = arriving[step, pl.ds(which * CAP, CAP)]

    def receive(step):
        @pl.when(has_far)
        def _():
            for piece in range(PIECES):
                at = piece * CHUNK
                arrived(step, NEAR, at, CHUNK, near_sem.at[step, piece])
                remote(section(step, NEAR, at, CHUNK), section(step, PASSED, at, CHUNK), 3, step, sibling,
                       other_sem.at[step, 2]).start()
            keep(step, NEAR)

        arrived(step, SIBLING, 0, CAP, other_sem.at[step, 0])
        keep(step, SIBLING)

        @pl.when(has_near)
        def _():
            arrived(step, FAR, 0, CAP, other_sem.at[step, 1])
            keep(step, FAR)
            arrived(step, PASSED, 0, CAP, other_sem.at[step, 2])
            keep(step, PASSED)

    def paired(lefts, blocks):
        both = lax.dot_general(
            jnp.concatenate(lefts, axis=0), jnp.concatenate(blocks, axis=0),
            (((1,), (1,)), ((), ())), preferred_element_type=jnp.float32,
        )
        height, width = lefts[0].shape[0], blocks[0].shape[0]
        return both[:height, :width], both[height:, width:]

    def solve(step, level, inverted):
        def pair(s):
            ats = [(step - 1) * CAP + s + t for t in range(2)]
            two = [table[ROW, at] for at in ats]
            lefts = [jnp.concatenate([solved[table[k, at]] for k in range(NEIGH)], axis=1) for at in ats]
            blocks = [jnp.concatenate([off[row, k] for k in range(NEIGH)], axis=1) for row in two]
            news = [
                (value[level * CAP + s + t].astype(jnp.float32) - total).astype(jnp.bfloat16)
                for t, total in enumerate(paired(lefts, blocks))
            ]
            if inverted:
                news = [new.astype(jnp.bfloat16) for new in paired(news, [inverse[row] for row in two])]
            return news

        def send(piece, last):
            send_near(step, piece)
            if last:
                send_far(step, (piece - 1) * CHUNK, 2 * CHUNK)

        def half(h, _):
            for p in range(PIECES // 2):
                piece = h * (PIECES // 2) + p
                news = sum([pair(piece * CHUNK + t) for t in range(0, CHUNK, 2)], [])
                for t, new in enumerate(news):
                    s = piece * CHUNK + t
                    value[level * CAP + s] = new
                    leaving[step, s] = new
                    solved[step * SPAN + OWN * CAP + s] = new
                act = functools.partial(send, piece, p == PIECES // 2 - 1)
                if inverted:
                    pl.when(step < STEPS)(act)
                else:
                    act()
            return 0

        lax.fori_loop(0, 2, half, 0)
        if inverted:
            pl.when(step < STEPS)(lambda: send_sibling(step))
        else:
            send_sibling(step)

    def place_values(level, number, first):
        for t in range(CAP):
            here = right[table[ROW, number * CAP + t]]
            value[level * CAP + t] = here
            if first:
                leaving[0, t] = here
                solved[OWN * CAP + t] = here

    load_table.wait()
    load_right.wait()
    place_values(0, 5, True)
    pl.semaphore_wait(barrier, 1 + has_near.astype(jnp.int32) + has_far.astype(jnp.int32))
    for piece in range(PIECES):
        send_near(0, piece)
    send_far(0, 0, CAP)
    send_sibling(0)
    fill_terms(me, parity, count, level_ref, neighbor_ref, rows, place, table_v)
    load_table.start()
    load_table.wait()
    for level in (1, 2, 3):
        place_values(level, level - 1, False)
    load_off.wait()
    load_inverse.wait()

    def forward_step(step, _):
        receive(step - 1)
        solve(step, step, False)
        return 0

    def backward_step(step, _):
        receive(step - 1)
        solve(step, STEPS - step, True)
        return 0

    lax.fori_loop(1, 3, forward_step, 0)
    lax.fori_loop(3, STEPS + 1, backward_step, 0)

    for i in range(rows):
        out_ref[i] = value[table[PLACE, i]]

    def sent(kind):
        def one(step, _):
            there = section(step, SIBLING)
            remote(there, there, kind, step, sibling, near_sem.at[step, 0]).wait_send()
            return 0

        lax.fori_loop(0, STEPS, one, 0)

    sent(0)

    @pl.when(has_near)
    def _():
        sent(1)

    @pl.when(has_far)
    def _():
        sent(2)
        sent(3)


def local(count, right_sides, off_blocks, diag_inv, neighbors, level_of):
    width, blk = right_sides.shape[1:]

    def slots(*sizes):
        return pltpu.VMEM((*sizes, width, blk), jnp.bfloat16)

    return pl.pallas_call(
        functools.partial(kernel, count),
        out_shape=pltpu.VMEM(right_sides.shape, jnp.bfloat16),
        in_specs=[pl.BlockSpec(memory_space=pltpu.VMEM)] * 2 + [pl.BlockSpec(memory_space=pl.ANY)] * 3,
        out_specs=pl.BlockSpec(memory_space=pltpu.VMEM),
        scratch_shapes=[
            pltpu.VMEM(right_sides.shape, jnp.bfloat16),
            pltpu.VMEM(off_blocks.shape, jnp.bfloat16),
            pltpu.VMEM(diag_inv.shape, jnp.bfloat16),
            pltpu.VMEM((8, 128), jnp.int32),
            pltpu.SMEM((8, 128), jnp.int32),
            slots(LEVELS * CAP),
            slots((STEPS + 1) * SPAN),
            slots(STEPS + 1, CAP),
            slots(STEPS, 4 * CAP),
            pltpu.SemaphoreType.DMA((4,)),
            pltpu.SemaphoreType.DMA((4, STEPS)),
            pltpu.SemaphoreType.DMA((STEPS, PIECES)),
            pltpu.SemaphoreType.DMA((STEPS, 3)),
        ],
        compiler_params=pltpu.CompilerParams(
            collective_id=0, has_side_effects=True, vmem_limit_bytes=56 * 1024 * 1024
        ),
        cost_estimate=pl.CostEstimate(flops=600_000_000, bytes_accessed=7_000_000, transcendentals=0),
    )(level_of.reshape(-1, 128), neighbors.T, right_sides, off_blocks, diag_inv)


def solution(mesh):
    in_specs = (
        P("space", "rhs", None),
        P("space", None, None, None),
        P("space", None, None),
        P("space", None),
        P(),
    )
    return jax.shard_map(
        functools.partial(local, mesh.shape["space"]),
        mesh=mesh, in_specs=in_specs, out_specs=P("space", "rhs", None), check_vma=False,
    )
```

time: 182 us -> 54.7 us (0.30)
  the two profiles are of different devices: /device:TPU:190 before, /device:TPU:262 now
where the time goes in v1:
time: 54.7 us; the launch traced here: 54.5 us
  Pallas kernels  53.8 us (98%)
  local copies, waits for them, and re-layouts  0.71 us (1%)
    pallas_call x1, Pallas kernels, local(): pl.pallas_call(functools.partial(kernel, count), out_shape=pltpu.VMEM(rig...  53.8 us

profile of v1, /device:TPU:262, one launch (start us, length us, event | category | flops | bytes accessed | tf_op | source)
XLA Modules:
  0.0 54.5 jit_solution(18125861126588759836)
XLA Ops:
  0.0 53.8 %shard_map.55 = bf16[32,32,128]{2,1,0:T(8,128)(2,1)S(1)} custom-call(s32[32,128]{1,0:T(8,128)} %bitcast.2, s32[5,32]{1,0:T(8,128)} %bitcast.3, bf16[32,32,128]{2,1,0:T(8,128)(2,1)} %right_hbm.1, bf16[32,5,128,128]{3,2,1,0:T(8,128)(2,1)} %off_hbm.1, bf16[32,128,128]{2,1,0:T(8,128)(2,1)} %inverse_hbm.1), custom_call_target="tpu_custom_call" | custom-call | flops 600000000 | bytes 7000000 | tf_op jit(solution)/shard_map/pallas_call | solution.py:299
  53.8 0.7 %copy.7 = bf16[32,32,128]{2,1,0:T(8,128)(2,1)} copy(bf16[32,32,128]{2,1,0:T(8,128)(2,1)S(1)} %shard_map.55) | data formatting | bytes 524288

commit v2 on v1

--- a/solution.py
+++ b/solution.py
@@ -89,9 +89,11 @@
         table_ref[k : k + 1, :] = jnp.clip(index, 0, ZERO)
 
 
-def kernel(count, level_ref, neighbor_ref, right_hbm, off_hbm, inverse_hbm, out_ref,
-           right, off, inverse, table_v, table, value, solved, leaving, arriving,
+def kernel(count, level_hbm, neighbor_hbm, right_hbm, off_hbm, inverse_hbm, out_ref,
+           level_ref, neighbor_ref, right, off, inverse, table_v, table, value, solved, leaving, arriving,
            load_sem, send_sem, near_sem, other_sem):
+    load_level = pltpu.make_async_copy(level_hbm, level_ref, load_sem.at[4])
+    load_level.start()
     me = lax.axis_index("space")
     parity = lax.rem(me, 2)
     sibling = me + 1 - 2 * parity
@@ -112,6 +114,8 @@
     rows = right.shape[0]
     load_right = pltpu.make_async_copy(right_hbm, right, load_sem.at[0])
     load_right.start()
+    load_neighbor = pltpu.make_async_copy(neighbor_hbm, neighbor_ref, load_sem.at[5])
+    load_neighbor.start()
     for start in range(0, rows, 4):
         part = pl.ds(start, 4)
         pltpu.make_async_copy(off_hbm.at[part], off.at[part], load_sem.at[1]).start()
@@ -121,6 +125,7 @@
     load_table = pltpu.make_async_copy(table_v, table, load_sem.at[3])
 
     table_v[...] = jnp.zeros_like(table_v)
+    load_level.wait()
     place = fill_rows(me, count, level_ref, rows, table_v)
     load_table.start()
     solved[ZERO] = jnp.zeros(solved.shape[1:], solved.dtype)
@@ -145,14 +150,28 @@
             remote(own(step, at, CHUNK), section(step, NEAR, at, CHUNK), 1, step, to_near,
                    near_sem.at[step, piece]).start()
 
-    def send_far(step, start, size):
+    def send_rest(step):
         @pl.when(has_far)
         def _():
-            remote(own(step, start, size), section(step, FAR, start, size), 2, step, to_far,
-                   other_sem.at[step, 1]).start()
-
-    def send_sibling(step):
+            remote(own(step), section(step, FAR), 2, step, to_far, other_sem.at[step, 1]).start()
+
         remote(own(step), section(step, SIBLING), 0, step, sibling, other_sem.at[step, 0]).start()
+
+    def sent(step):
+        def wait(kind):
+            there = section(step, SIBLING)
+            remote(there, there, kind, step, sibling, near_sem.at[step, 0]).wait_send()
+
+        wait(0)
+
+        @pl.when(has_near)
+        def _():
+            wait(1)
+
+        @pl.when(has_far)
+        def _():
+            wait(2)
+            wait(3)
 
     def arrived(step, which, start, size, sem):
         there = section(step, which, start, size)
@@ -203,11 +222,6 @@
                 news = [new.astype(jnp.bfloat16) for new in paired(news, [inverse[row] for row in two])]
             return news
 
-        def send(piece, last):
-            send_near(step, piece)
-            if last:
-                send_far(step, (piece - 1) * CHUNK, 2 * CHUNK)
-
         def half(h, _):
             for p in range(PIECES // 2):
                 piece = h * (PIECES // 2) + p
@@ -217,18 +231,18 @@
                     value[level * CAP + s] = new
                     leaving[step, s] = new
                     solved[step * SPAN + OWN * CAP + s] = new
-                act = functools.partial(send, piece, p == PIECES // 2 - 1)
                 if inverted:
-                    pl.when(step < STEPS)(act)
+                    pl.when(step < STEPS)(functools.partial(send_near, step, piece))
                 else:
-                    act()
+                    send_near(step, piece)
             return 0
 
         lax.fori_loop(0, 2, half, 0)
         if inverted:
-            pl.when(step < STEPS)(lambda: send_sibling(step))
+            pl.when(step < STEPS)(functools.partial(send_rest, step))
         else:
-            send_sibling(step)
+            send_rest(step)
+        sent(step - 1)
 
     def place_values(level, number, first):
         for t in range(CAP):
@@ -244,8 +258,8 @@
     pl.semaphore_wait(barrier, 1 + has_near.astype(jnp.int32) + has_far.astype(jnp.int32))
     for piece in range(PIECES):
         send_near(0, piece)
-    send_far(0, 0, CAP)
-    send_sibling(0)
+    send_rest(0)
+    load_neighbor.wait()
     fill_terms(me, parity, count, level_ref, neighbor_ref, rows, place, table_v)
     load_table.start()
     load_table.wait()
@@ -270,25 +284,6 @@
     for i in range(rows):
         out_ref[i] = value[table[PLACE, i]]
 
-    def sent(kind):
-        def one(step, _):
-            there = section(step, SIBLING)
-            remote(there, there, kind, step, sibling, near_sem.at[step, 0]).wait_send()
-            return 0
-
-        lax.fori_loop(0, STEPS, one, 0)
-
-    sent(0)
-
-    @pl.when(has_near)
-    def _():
-        sent(1)
-
-    @pl.when(has_far)
-    def _():
-        sent(2)
-        sent(3)
-
 
 def local(count, right_sides, off_blocks, diag_inv, neighbors, level_of):
     width, blk = right_sides.shape[1:]
@@ -299,9 +294,11 @@
     return pl.pallas_call(
         functools.partial(kernel, count),
         out_shape=pltpu.VMEM(right_sides.shape, jnp.bfloat16),
-        in_specs=[pl.BlockSpec(memory_space=pltpu.VMEM)] * 2 + [pl.BlockSpec(memory_space=pl.ANY)] * 3,
+        in_specs=[pl.BlockSpec(memory_space=pl.ANY)] * 5,
         out_specs=pl.BlockSpec(memory_space=pltpu.VMEM),
         scratch_shapes=[
+            pltpu.VMEM((level_of.shape[0] // 128, 128), jnp.int32),
+            pltpu.VMEM(neighbors.shape[::-1], jnp.int32),
             pltpu.VMEM(right_sides.shape, jnp.bfloat16),
             pltpu.VMEM(off_blocks.shape, jnp.bfloat16),
             pltpu.VMEM(diag_inv.shape, jnp.bfloat16),
@@ -311,7 +308,7 @@
             slots((STEPS + 1) * SPAN),
             slots(STEPS + 1, CAP),
             slots(STEPS, 4 * CAP),
-            pltpu.SemaphoreType.DMA((4,)),
+            pltpu.SemaphoreType.DMA((6,)),
             pltpu.SemaphoreType.DMA((4, STEPS)),
             pltpu.SemaphoreType.DMA((STEPS, PIECES)),
             pltpu.SemaphoreType.DMA((STEPS, 3)),

time: 54.7 us -> 55.3 us (1.011)
  the two profiles are of different devices: /device:TPU:262 before, /device:TPU:255 now
where the time goes in v2:
time: 55.3 us; the launch traced here: 55.2 us
  Pallas kernels  54.4 us (98%)
  local copies, waits for them, and re-layouts  0.71 us (1%)
    pallas_call x1, Pallas kernels, local(): pl.pallas_call(functools.partial(kernel, count), out_shape=pltpu.VMEM(rig...  54.4 us

profile of v2, /device:TPU:255, one launch (start us, length us, event | category | flops | bytes accessed | tf_op | source)
XLA Modules:
  0.0 55.2 jit_solution(1256506807698224655)
XLA Ops:
  0.0 54.4 %shard_map.55 = bf16[32,32,128]{2,1,0:T(8,128)(2,1)S(1)} custom-call(s32[32,128]{1,0:T(8,128)} %bitcast.2, s32[5,32]{1,0:T(8,128)} %bitcast.3, bf16[32,32,128]{2,1,0:T(8,128)(2,1)} %right_hbm.1, bf16[32,5,128,128]{3,2,1,0:T(8,128)(2,1)} %off_hbm.1, bf16[32,128,128]{2,1,0:T(8,128)(2,1)} %inverse_hbm.1), custom_call_target="tpu_custom_call" | custom-call | flops 600000000 | bytes 7000000 | tf_op jit(solution)/shard_map/pallas_call | solution.py:294
  54.4 0.7 %copy.7 = bf16[32,32,128]{2,1,0:T(8,128)(2,1)} copy(bf16[32,32,128]{2,1,0:T(8,128)(2,1)S(1)} %shard_map.55) | data formatting | bytes 524288

commit v3 on v2

--- a/solution.py
+++ b/solution.py
@@ -15,6 +15,7 @@
 STEPS = 6
 CHUNK = 4
 PIECES = CAP // CHUNK
+PASSED_ON = 3
 SIBLING, NEAR, FAR, PASSED, OWN = range(5)
 SPAN = 5 * CAP
 ZERO = STEPS * SPAN
@@ -97,7 +98,7 @@
     me = lax.axis_index("space")
     parity = lax.rem(me, 2)
     sibling = me + 1 - 2 * parity
-    to_near, to_far = me - 2 + 4 * parity, me + 2 - 4 * parity
+    to_near, to_cross, to_far = me - 2 + 4 * parity, me - 1 + 2 * parity, me + 2 - 4 * parity
     has_near = (to_near >= 0) & (to_near < count)
     has_far = (to_far >= 0) & (to_far < count)
 
@@ -108,7 +109,7 @@
             pl.semaphore_signal(barrier, inc=1, device_id={"space": target}, device_id_type=MESH)
 
     greet(sibling)
-    pl.when(has_near)(lambda: greet(to_near))
+    pl.when(has_near)(lambda: greet(to_near, to_cross))
     pl.when(has_far)(lambda: greet(to_far))
 
     rows = right.shape[0]
@@ -150,6 +151,11 @@
             remote(own(step, at, CHUNK), section(step, NEAR, at, CHUNK), 1, step, to_near,
                    near_sem.at[step, piece]).start()
 
+            @pl.when(piece >= PASSED_ON)
+            def _():
+                remote(own(step, at, CHUNK), section(step, PASSED, at, CHUNK), 4, step, to_cross,
+                       other_sem.at[step, 3]).start()
+
     def send_rest(step):
         @pl.when(has_far)
         def _():
@@ -158,8 +164,8 @@
         remote(own(step), section(step, SIBLING), 0, step, sibling, other_sem.at[step, 0]).start()
 
     def sent(step):
-        def wait(kind):
-            there = section(step, SIBLING)
+        def wait(kind, pieces=PIECES):
+            there = section(step, SIBLING, 0, pieces * CHUNK)
             remote(there, there, kind, step, sibling, near_sem.at[step, 0]).wait_send()
 
         wait(0)
@@ -167,11 +173,12 @@
         @pl.when(has_near)
         def _():
             wait(1)
+            wait(4, PIECES - PASSED_ON)
 
         @pl.when(has_far)
         def _():
             wait(2)
-            wait(3)
+            wait(3, PASSED_ON)
 
     def arrived(step, which, start, size, sem):
         there = section(step, which, start, size)
@@ -186,8 +193,9 @@
             for piece in range(PIECES):
                 at = piece * CHUNK
                 arrived(step, NEAR, at, CHUNK, near_sem.at[step, piece])
-                remote(section(step, NEAR, at, CHUNK), section(step, PASSED, at, CHUNK), 3, step, sibling,
-                       other_sem.at[step, 2]).start()
+                if piece < PASSED_ON:
+                    remote(section(step, NEAR, at, CHUNK), section(step, PASSED, at, CHUNK), 3, step, sibling,
+                           other_sem.at[step, 2]).start()
             keep(step, NEAR)
 
         arrived(step, SIBLING, 0, CAP, other_sem.at[step, 0])
@@ -197,7 +205,8 @@
         def _():
             arrived(step, FAR, 0, CAP, other_sem.at[step, 1])
             keep(step, FAR)
-            arrived(step, PASSED, 0, CAP, other_sem.at[step, 2])
+            arrived(step, PASSED, 0, PASSED_ON * CHUNK, other_sem.at[step, 2])
+            arrived(step, PASSED, PASSED_ON * CHUNK, CAP - PASSED_ON * CHUNK, other_sem.at[step, 3])
             keep(step, PASSED)
 
     def paired(lefts, blocks):
@@ -255,7 +264,7 @@
     load_table.wait()
     load_right.wait()
     place_values(0, 5, True)
-    pl.semaphore_wait(barrier, 1 + has_near.astype(jnp.int32) + has_far.astype(jnp.int32))
+    pl.semaphore_wait(barrier, 1 + 2 * has_near.astype(jnp.int32) + has_far.astype(jnp.int32))
     for piece in range(PIECES):
         send_near(0, piece)
     send_rest(0)
@@ -309,9 +318,9 @@
             slots(STEPS + 1, CAP),
             slots(STEPS, 4 * CAP),
             pltpu.SemaphoreType.DMA((6,)),
-            pltpu.SemaphoreType.DMA((4, STEPS)),
+            pltpu.SemaphoreType.DMA((5, STEPS)),
             pltpu.SemaphoreType.DMA((STEPS, PIECES)),
-            pltpu.SemaphoreType.DMA((STEPS, 3)),
+            pltpu.SemaphoreType.DMA((STEPS, 4)),
         ],
         compiler_params=pltpu.CompilerParams(
             collective_id=0, has_side_effects=True, vmem_limit_bytes=56 * 1024 * 1024

time: 55.3 us -> 55.1 us (level)
  no operation moved by 1% of the time
where the time goes in v3:
time: 55.1 us; the launch traced here: 54.9 us
  Pallas kernels  54.2 us (98%)
  local copies, waits for them, and re-layouts  0.71 us (1%)
    pallas_call x1, Pallas kernels, local(): pl.pallas_call(functools.partial(kernel, count), out_shape=pltpu.VMEM(rig...  54.2 us

profile of v3, /device:TPU:255, one launch (start us, length us, event | category | flops | bytes accessed | tf_op | source)
XLA Modules:
  0.0 54.9 jit_solution(16894152161453471720)
XLA Ops:
  0.0 54.2 %shard_map.55 = bf16[32,32,128]{2,1,0:T(8,128)(2,1)S(1)} custom-call(s32[32,128]{1,0:T(8,128)} %bitcast.2, s32[5,32]{1,0:T(8,128)} %bitcast.3, bf16[32,32,128]{2,1,0:T(8,128)(2,1)} %right_hbm.1, bf16[32,5,128,128]{3,2,1,0:T(8,128)(2,1)} %off_hbm.1, bf16[32,128,128]{2,1,0:T(8,128)(2,1)} %inverse_hbm.1), custom_call_target="tpu_custom_call" | custom-call | flops 600000000 | bytes 7000000 | tf_op jit(solution)/shard_map/pallas_call | solution.py:303
  54.2 0.7 %copy.7 = bf16[32,32,128]{2,1,0:T(8,128)(2,1)} copy(bf16[32,32,128]{2,1,0:T(8,128)(2,1)S(1)} %shard_map.55) | data formatting | bytes 524288

commit v4 on v2

--- a/solution.py
+++ b/solution.py
@@ -16,6 +16,7 @@
 CHUNK = 4
 PIECES = CAP // CHUNK
 SIBLING, NEAR, FAR, PASSED, OWN = range(5)
+SPARE = 4
 SPAN = 5 * CAP
 ZERO = STEPS * SPAN
 ROW, PLACE = NEIGH, NEIGH + 1
@@ -101,6 +102,12 @@
     has_near = (to_near >= 0) & (to_near < count)
     has_far = (to_far >= 0) & (to_far < count)
 
+    near_there, far_there = has_near.astype(jnp.int32), has_far.astype(jnp.int32)
+    near_to = sibling + near_there * (to_near - sibling)
+    near_at = (SPARE + near_there * (NEAR - SPARE)) * CAP
+    far_to = sibling + far_there * (to_far - sibling)
+    far_at = (SPARE + far_there * (FAR - SPARE)) * CAP
+
     barrier = pltpu.get_barrier_semaphore()
 
     def greet(*targets):
@@ -144,17 +151,14 @@
 
     def send_near(step, piece):
         at = piece * CHUNK
-
-        @pl.when(has_near)
-        def _():
-            remote(own(step, at, CHUNK), section(step, NEAR, at, CHUNK), 1, step, to_near,
-                   near_sem.at[step, piece]).start()
-
-    def send_rest(step):
-        @pl.when(has_far)
-        def _():
-            remote(own(step), section(step, FAR), 2, step, to_far, other_sem.at[step, 1]).start()
-
+        remote(own(step, at, CHUNK), arriving.at[step, pl.ds(near_at + at, CHUNK)], 1, step, near_to,
+               near_sem.at[step, near_there * piece + (1 - near_there) * PIECES]).start()
+
+    def send_far(step, start, size):
+        remote(own(step, start, size), arriving.at[step, pl.ds(far_at + start, size)], 2, step, far_to,
+               other_sem.at[step, 3 - 2 * far_there]).start()
+
+    def send_sibling(step):
         remote(own(step), section(step, SIBLING), 0, step, sibling, other_sem.at[step, 0]).start()
 
     def sent(step):
@@ -163,15 +167,9 @@
             remote(there, there, kind, step, sibling, near_sem.at[step, 0]).wait_send()
 
         wait(0)
-
-        @pl.when(has_near)
-        def _():
-            wait(1)
-
-        @pl.when(has_far)
-        def _():
-            wait(2)
-            wait(3)
+        wait(1)
+        wait(2)
+        pl.when(has_far)(lambda: wait(3))
 
     def arrived(step, which, start, size, sem):
         there = section(step, which, start, size)
@@ -190,6 +188,14 @@
                        other_sem.at[step, 2]).start()
             keep(step, NEAR)
 
+        @pl.when(jnp.logical_not(has_far))
+        def _():
+            arrived(step, SPARE, 0, CAP, near_sem.at[step, PIECES])
+
+        @pl.when(jnp.logical_not(has_near))
+        def _():
+            arrived(step, SPARE, 0, CAP, other_sem.at[step, 3])
+
         arrived(step, SIBLING, 0, CAP, other_sem.at[step, 0])
         keep(step, SIBLING)
 
@@ -208,7 +214,7 @@
         height, width = lefts[0].shape[0], blocks[0].shape[0]
         return both[:height, :width], both[height:, width:]
 
-    def solve(step, level, inverted):
+    def solve(step, level, inverted, leaves):
         def pair(s):
             ats = [(step - 1) * CAP + s + t for t in range(2)]
             two = [table[ROW, at] for at in ats]
@@ -222,26 +228,22 @@
                 news = [new.astype(jnp.bfloat16) for new in paired(news, [inverse[row] for row in two])]
             return news
 
-        def half(h, _):
-            for p in range(PIECES // 2):
-                piece = h * (PIECES // 2) + p
-                news = sum([pair(piece * CHUNK + t) for t in range(0, CHUNK, 2)], [])
-                for t, new in enumerate(news):
-                    s = piece * CHUNK + t
-                    value[level * CAP + s] = new
-                    leaving[step, s] = new
-                    solved[step * SPAN + OWN * CAP + s] = new
-                if inverted:
-                    pl.when(step < STEPS)(functools.partial(send_near, step, piece))
-                else:
-                    send_near(step, piece)
-            return 0
-
-        lax.fori_loop(0, 2, half, 0)
-        if inverted:
-            pl.when(step < STEPS)(functools.partial(send_rest, step))
-        else:
-            send_rest(step)
+        everything = []
+        for piece in range(PIECES):
+            news = sum([pair(piece * CHUNK + t) for t in range(0, CHUNK, 2)], [])
+            for t, new in enumerate(news):
+                value[level * CAP + piece * CHUNK + t] = new
+                if leaves:
+                    leaving[step, piece * CHUNK + t] = new
+            everything += news
+            if leaves:
+                send_near(step, piece)
+                if piece % 2 == 1:
+                    send_far(step, (piece - 1) * CHUNK, 2 * CHUNK)
+        if leaves:
+            send_sibling(step)
+            for t, new in enumerate(everything):
+                solved[step * SPAN + OWN * CAP + t] = new
         sent(step - 1)
 
     def place_values(level, number, first):
@@ -258,7 +260,8 @@
     pl.semaphore_wait(barrier, 1 + has_near.astype(jnp.int32) + has_far.astype(jnp.int32))
     for piece in range(PIECES):
         send_near(0, piece)
-    send_rest(0)
+    send_far(0, 0, CAP)
+    send_sibling(0)
     load_neighbor.wait()
     fill_terms(me, parity, count, level_ref, neighbor_ref, rows, place, table_v)
     load_table.start()
@@ -270,16 +273,18 @@
 
     def forward_step(step, _):
         receive(step - 1)
-        solve(step, step, False)
+        solve(step, step, False, True)
         return 0
 
     def backward_step(step, _):
         receive(step - 1)
-        solve(step, STEPS - step, True)
+        solve(step, STEPS - step, True, True)
         return 0
 
     lax.fori_loop(1, 3, forward_step, 0)
-    lax.fori_loop(3, STEPS + 1, backward_step, 0)
+    lax.fori_loop(3, STEPS, backward_step, 0)
+    receive(STEPS - 1)
+    solve(STEPS, 0, True, False)
 
     for i in range(rows):
         out_ref[i] = value[table[PLACE, i]]
@@ -305,13 +310,13 @@
             pltpu.VMEM((8, 128), jnp.int32),
             pltpu.SMEM((8, 128), jnp.int32),
             slots(LEVELS * CAP),
-            slots((STEPS + 1) * SPAN),
-            slots(STEPS + 1, CAP),
-            slots(STEPS, 4 * CAP),
+            slots(STEPS * SPAN + 1),
+            slots(STEPS, CAP),
+            slots(STEPS, 5 * CAP),
             pltpu.SemaphoreType.DMA((6,)),
             pltpu.SemaphoreType.DMA((4, STEPS)),
-            pltpu.SemaphoreType.DMA((STEPS, PIECES)),
-            pltpu.SemaphoreType.DMA((STEPS, 3)),
+            pltpu.SemaphoreType.DMA((STEPS, PIECES + 1)),
+            pltpu.SemaphoreType.DMA((STEPS, 4)),
         ],
         compiler_params=pltpu.CompilerParams(
             collective_id=0, has_side_effects=True, vmem_limit_bytes=56 * 1024 * 1024

time: 55.3 us -> 53.7 us (0.971)
  Pallas kernels: 54.4 us -> 52.8 us
    pallas_call x1, Pallas kernels: 54.4 us -> 52.8 us  [local(): pl.pallas_call(functools.partial(kernel, count), out_shape=pltpu.VMEM(rig...]
where the time goes in v4:
time: 53.7 us; the launch traced here: 53.5 us
  Pallas kernels  52.8 us (98%)
  local copies, waits for them, and re-layouts  0.71 us (1%)
    pallas_call x1, Pallas kernels, local(): pl.pallas_call(functools.partial(kernel, count), out_shape=pltpu.VMEM(rig...  52.8 us

profile of v4, /device:TPU:255, one launch (start us, length us, event | category | flops | bytes accessed | tf_op | source)
XLA Modules:
  0.0 53.5 jit_solution(4365388146722716969)
XLA Ops:
  0.0 52.8 %shard_map.55 = bf16[32,32,128]{2,1,0:T(8,128)(2,1)S(1)} custom-call(s32[32,128]{1,0:T(8,128)} %bitcast.2, s32[5,32]{1,0:T(8,128)} %bitcast.3, bf16[32,32,128]{2,1,0:T(8,128)(2,1)} %right_hbm.1, bf16[32,5,128,128]{3,2,1,0:T(8,128)(2,1)} %off_hbm.1, bf16[32,128,128]{2,1,0:T(8,128)(2,1)} %inverse_hbm.1), custom_call_target="tpu_custom_call" | custom-call | flops 600000000 | bytes 7000000 | tf_op jit(solution)/shard_map/pallas_call | solution.py:299
  52.8 0.7 %copy.7 = bf16[32,32,128]{2,1,0:T(8,128)(2,1)} copy(bf16[32,32,128]{2,1,0:T(8,128)(2,1)S(1)} %shard_map.55) | data formatting | bytes 524288

commit v5 on v4

--- a/solution.py
+++ b/solution.py
@@ -15,6 +15,7 @@
 STEPS = 6
 CHUNK = 4
 PIECES = CAP // CHUNK
+COPY = 2
 SIBLING, NEAR, FAR, PASSED, OWN = range(5)
 SPARE = 4
 SPAN = 5 * CAP
@@ -149,14 +150,13 @@
     def own(step, start=0, size=CAP):
         return leaving.at[step, pl.ds(start, size)]
 
-    def send_near(step, piece):
-        at = piece * CHUNK
-        remote(own(step, at, CHUNK), arriving.at[step, pl.ds(near_at + at, CHUNK)], 1, step, near_to,
-               near_sem.at[step, near_there * piece + (1 - near_there) * PIECES]).start()
-
-    def send_far(step, start, size):
-        remote(own(step, start, size), arriving.at[step, pl.ds(far_at + start, size)], 2, step, far_to,
-               other_sem.at[step, 3 - 2 * far_there]).start()
+    def send_piece(step, piece):
+        for at in range(piece * CHUNK, (piece + 1) * CHUNK, COPY):
+            remote(own(step, at, COPY), arriving.at[step, pl.ds(near_at + at, COPY)], 1, step, near_to,
+                   near_sem.at[step, near_there * piece + (1 - near_there) * PIECES]).start()
+        for at in range(piece * CHUNK, (piece + 1) * CHUNK, COPY):
+            remote(own(step, at, COPY), arriving.at[step, pl.ds(far_at + at, COPY)], 2, step, far_to,
+                   other_sem.at[step, 3 - 2 * far_there]).start()
 
     def send_sibling(step):
         remote(own(step), section(step, SIBLING), 0, step, sibling, other_sem.at[step, 0]).start()
@@ -237,9 +237,7 @@
                     leaving[step, piece * CHUNK + t] = new
             everything += news
             if leaves:
-                send_near(step, piece)
-                if piece % 2 == 1:
-                    send_far(step, (piece - 1) * CHUNK, 2 * CHUNK)
+                send_piece(step, piece)
         if leaves:
             send_sibling(step)
             for t, new in enumerate(everything):
@@ -259,8 +257,7 @@
     place_values(0, 5, True)
     pl.semaphore_wait(barrier, 1 + has_near.astype(jnp.int32) + has_far.astype(jnp.int32))
     for piece in range(PIECES):
-        send_near(0, piece)
-    send_far(0, 0, CAP)
+        send_piece(0, piece)
     send_sibling(0)
     load_neighbor.wait()
     fill_terms(me, parity, count, level_ref, neighbor_ref, rows, place, table_v)

time: 53.7 us -> 52.4 us (0.976)
  Pallas kernels: 52.8 us -> 51.5 us
    pallas_call x1, Pallas kernels: 52.8 us -> 51.5 us  [local(): pl.pallas_call(functools.partial(kernel, count), out_shape=pltpu.VMEM(rig...]
where the time goes in v5:
time: 52.4 us; the launch traced here: 52.2 us
  Pallas kernels  51.5 us (98%)
  local copies, waits for them, and re-layouts  0.71 us (1%)
    pallas_call x1, Pallas kernels, local(): pl.pallas_call(functools.partial(kernel, count), out_shape=pltpu.VMEM(rig...  51.5 us

profile of v5, /device:TPU:255, one launch (start us, length us, event | category | flops | bytes accessed | tf_op | source)
XLA Modules:
  0.0 52.2 jit_solution(11782967976770968494)
XLA Ops:
  0.0 51.5 %shard_map.55 = bf16[32,32,128]{2,1,0:T(8,128)(2,1)S(1)} custom-call(s32[32,128]{1,0:T(8,128)} %bitcast.2, s32[5,32]{1,0:T(8,128)} %bitcast.3, bf16[32,32,128]{2,1,0:T(8,128)(2,1)} %right_hbm.1, bf16[32,5,128,128]{3,2,1,0:T(8,128)(2,1)} %off_hbm.1, bf16[32,128,128]{2,1,0:T(8,128)(2,1)} %inverse_hbm.1), custom_call_target="tpu_custom_call" | custom-call | flops 600000000 | bytes 7000000 | tf_op jit(solution)/shard_map/pallas_call | solution.py:296
  51.5 0.7 %copy.7 = bf16[32,32,128]{2,1,0:T(8,128)(2,1)} copy(bf16[32,32,128]{2,1,0:T(8,128)(2,1)S(1)} %shard_map.55) | data formatting | bytes 524288

commit v6 on v5

--- a/solution.py
+++ b/solution.py
@@ -157,9 +157,9 @@
         for at in range(piece * CHUNK, (piece + 1) * CHUNK, COPY):
             remote(own(step, at, COPY), arriving.at[step, pl.ds(far_at + at, COPY)], 2, step, far_to,
                    other_sem.at[step, 3 - 2 * far_there]).start()
-
-    def send_sibling(step):
-        remote(own(step), section(step, SIBLING), 0, step, sibling, other_sem.at[step, 0]).start()
+        at = piece * CHUNK
+        remote(own(step, at, CHUNK), section(step, SIBLING, at, CHUNK), 0, step, sibling,
+               other_sem.at[step, 0]).start()
 
     def sent(step):
         def wait(kind):
@@ -184,8 +184,9 @@
             for piece in range(PIECES):
                 at = piece * CHUNK
                 arrived(step, NEAR, at, CHUNK, near_sem.at[step, piece])
-                remote(section(step, NEAR, at, CHUNK), section(step, PASSED, at, CHUNK), 3, step, sibling,
-                       other_sem.at[step, 2]).start()
+                for start in range(at, at + CHUNK, COPY):
+                    remote(section(step, NEAR, start, COPY), section(step, PASSED, start, COPY), 3, step, sibling,
+                           other_sem.at[step, 2]).start()
             keep(step, NEAR)
 
         @pl.when(jnp.logical_not(has_far))
@@ -239,7 +240,6 @@
             if leaves:
                 send_piece(step, piece)
         if leaves:
-            send_sibling(step)
             for t, new in enumerate(everything):
                 solved[step * SPAN + OWN * CAP + t] = new
         sent(step - 1)
@@ -258,7 +258,6 @@
     pl.semaphore_wait(barrier, 1 + has_near.astype(jnp.int32) + has_far.astype(jnp.int32))
     for piece in range(PIECES):
         send_piece(0, piece)
-    send_sibling(0)
     load_neighbor.wait()
     fill_terms(me, parity, count, level_ref, neighbor_ref, rows, place, table_v)
     load_table.start()

time: 52.4 us -> 52.5 us (level)
  the two profiles are of different devices: /device:TPU:255 before, /device:TPU:253 now
where the time goes in v6:
time: 52.5 us; the launch traced here: 52.3 us
  Pallas kernels  51.6 us (98%)
  local copies, waits for them, and re-layouts  0.71 us (1%)
    pallas_call x1, Pallas kernels, local(): pl.pallas_call(functools.partial(kernel, count), out_shape=pltpu.VMEM(rig...  51.6 us

profile of v6, /device:TPU:253, one launch (start us, length us, event | category | flops | bytes accessed | tf_op | source)
XLA Modules:
  0.0 52.3 jit_solution(11766869999889190440)
XLA Ops:
  0.0 51.6 %shard_map.55 = bf16[32,32,128]{2,1,0:T(8,128)(2,1)S(1)} custom-call(s32[32,128]{1,0:T(8,128)} %bitcast.2, s32[5,32]{1,0:T(8,128)} %bitcast.3, bf16[32,32,128]{2,1,0:T(8,128)(2,1)} %right_hbm.1, bf16[32,5,128,128]{3,2,1,0:T(8,128)(2,1)} %off_hbm.1, bf16[32,128,128]{2,1,0:T(8,128)(2,1)} %inverse_hbm.1), custom_call_target="tpu_custom_call" | custom-call | flops 600000000 | bytes 7000000 | tf_op jit(solution)/shard_map/pallas_call | solution.py:295
  51.6 0.7 %copy.7 = bf16[32,32,128]{2,1,0:T(8,128)(2,1)} copy(bf16[32,32,128]{2,1,0:T(8,128)(2,1)S(1)} %shard_map.55) | data formatting | bytes 524288

commit v7 on v5

--- a/solution.py
+++ b/solution.py
@@ -15,7 +15,7 @@
 STEPS = 6
 CHUNK = 4
 PIECES = CAP // CHUNK
-COPY = 2
+COPY = 1
 SIBLING, NEAR, FAR, PASSED, OWN = range(5)
 SPARE = 4
 SPAN = 5 * CAP

time: 52.4 us -> 52.8 us (level)
  the two profiles are of different devices: /device:TPU:255 before, /device:TPU:249 now
where the time goes in v7:
time: 52.8 us; the launch traced here: 52.6 us
  Pallas kernels  51.9 us (98%)
  local copies, waits for them, and re-layouts  0.71 us (1%)
    pallas_call x1, Pallas kernels, local(): pl.pallas_call(functools.partial(kernel, count), out_shape=pltpu.VMEM(rig...  51.9 us

profile of v7, /device:TPU:249, one launch (start us, length us, event | category | flops | bytes accessed | tf_op | source)
XLA Modules:
  0.0 52.6 jit_solution(7080376961060027167)
XLA Ops:
  0.0 51.9 %shard_map.55 = bf16[32,32,128]{2,1,0:T(8,128)(2,1)S(1)} custom-call(s32[32,128]{1,0:T(8,128)} %bitcast.2, s32[5,32]{1,0:T(8,128)} %bitcast.3, bf16[32,32,128]{2,1,0:T(8,128)(2,1)} %right_hbm.1, bf16[32,5,128,128]{3,2,1,0:T(8,128)(2,1)} %off_hbm.1, bf16[32,128,128]{2,1,0:T(8,128)(2,1)} %inverse_hbm.1), custom_call_target="tpu_custom_call" | custom-call | flops 600000000 | bytes 7000000 | tf_op jit(solution)/shard_map/pallas_call | solution.py:296
  51.9 0.7 %copy.7 = bf16[32,32,128]{2,1,0:T(8,128)(2,1)} copy(bf16[32,32,128]{2,1,0:T(8,128)(2,1)S(1)} %shard_map.55) | data formatting | bytes 524288
